TPU v7x, 32 devices: a whole 2x2x4 slice. The times are simulated.
32 devices in a mesh: grp: 2 (over y), row: 4 (over z), col: 2 (over x), sub: 2 (over core).
Axes of the slice: x: 2, y: 2, z: 4, core: 2. Of those that a mesh axis runs over, the one named last changes fastest.
Arguments:
- samples: bfloat16 [512, 2, 16, 512], P(('grp', 'row', 'col', 'sub')), parts along dimension 0, may hold values from -6 to 6
- analysis_taps: float32 [16, 16], replicated, may hold values from -1 to 1
- synthesis_taps: float32 [16, 16], replicated, may hold values from -1 to 1
- antenna_station: int32 [512], P('grp'), parts along dimension 0, may hold values from 0 to 31, as said below
- station_group: int32 [64, 1], P('grp'), parts along dimension 0, may hold values from 0 to 7
- beam_group: int32 [2048], P('grp'), parts along dimension 0, may hold values from 0 to 7
- beam_weights: bfloat16 [32, 2, 1024, 32], P(('grp', 'row'), None, ('col', 'sub')), parts along dimension 0, may hold values from -6 to 6
Outputs:
- visibilities: float32 [16, 2, 64, 32], P('row', None, ('grp', 'col', 'sub')), parts along dimension 2
- beam_series: float32 [2048, 2, 16, 512], P(('grp', 'col', 'sub', 'row')), parts along dimension 0
There are 2 independent parts, one for each index of `grp`. A program takes and returns all parts, laid end to end along the dimension named above; an argument that names none is the same for every part. Nothing has to cross between parts.
Inputs may be any that keep to these rules, and one draw needn't show every extreme that they name: `antenna_station`: every station is named by exactly 8 antennas.
All inputs are finite; a program needn't handle non-finite values.
Results may differ from a plain program's by a relative error of at most 0.005.
Values may be sent and summed in bfloat16 or wider, within the bound.
A program may use at most 64 MiB of HBM per device.

v0:
```python
import math
import jax
import jax.numpy as jnp
from jax import lax
from jax.sharding import PartitionSpec as P

ANTENNAS_PER_STN = 8
SPEC = 512


def polyphase(signal, coefficients):
    length = signal.shape[-1]
    output = coefficients[0][:, None] * signal
    for tap_index in range(1, coefficients.shape[0]):
        shifted = jnp.pad(
            signal[..., : length - tap_index], [(0, 0)] * (signal.ndim - 1) + [(tap_index, 0)]
        )
        output = output + coefficients[tap_index][:, None] * shifted
    return output


def fourier_table(length, direction):
    indices = jnp.arange(length)
    angles = (
        2.0 * math.pi / length * (indices[:, None] * indices[None, :] % length).astype(jnp.float32)
    )
    cosine_part = jnp.cos(angles)
    sine_part = jnp.sin(angles)
    table = jnp.stack(
        [
            jnp.stack([cosine_part, direction * sine_part]),
            jnp.stack([-direction * sine_part, cosine_part]),
        ]
    )
    return table.transpose(0, 2, 1, 3) * (1.0 / math.sqrt(length))


def body(
    samples, analysis_taps, synthesis_taps, antenna_station, station_group, beam_group, beam_weights
):
    high = lax.Precision.HIGHEST
    block_count = lax.axis_size(("col", "sub"))
    block_index = lax.axis_index(("col", "sub"))
    filtered = polyphase(samples.astype(jnp.float32), analysis_taps)
    spectra = jnp.einsum(
        "aqcf,qcpk->apkf", filtered, fourier_table(samples.shape[2], -1.0), precision=high
    ).astype(jnp.bfloat16)
    turned = lax.all_to_all(spectra, "row", split_axis=2, concat_axis=0, tiled=True)
    local_count = spectra.shape[0]
    held_rows = turned.shape[0]
    chan_rows = turned.shape[2]
    spec_len = turned.shape[3]
    station_count = station_group.shape[0]
    flat_width = 2 * chan_rows * spec_len
    tile_rows = station_count // block_count
    shard_rows = lax.all_gather(turned, ("col", "sub"), axis=0, tiled=True)
    row_total = shard_rows.shape[0]
    positions = jnp.arange(row_total, dtype=jnp.int32)
    source_block = positions // held_rows
    offset_rows = positions % held_rows
    source_row = offset_rows // local_count
    antenna = offset_rows % local_count
    global_index = (source_row * block_count + source_block) * local_count + antenna
    targets = antenna_station[global_index]
    wanted = jnp.arange(station_count, dtype=jnp.int32)
    one_hot = (targets[None, :] == wanted[:, None]).astype(jnp.bfloat16)
    summed_values = jnp.dot(
        one_hot, shard_rows.reshape(row_total, flat_width), preferred_element_type=jnp.float32
    )
    flat_stations = (summed_values * (1.0 / math.sqrt(ANTENNAS_PER_STN))).astype(jnp.bfloat16)
    station_list = flat_stations.reshape(station_count, 2, chan_rows, spec_len)
    real_part = station_list[:, 0]
    imag_part = station_list[:, 1]
    own_rows = lax.dynamic_slice_in_dim(station_list, block_index * tile_rows, tile_rows, 0)
    own_real = own_rows[:, 0]
    own_imag = own_rows[:, 1]
    vis_real = (
        jnp.einsum("icf,jcf->cij", own_real, real_part, preferred_element_type=jnp.float32)
        + jnp.einsum("icf,jcf->cij", own_imag, imag_part, preferred_element_type=jnp.float32)
    ) * (1.0 / SPEC)
    vis_imag = (
        jnp.einsum("icf,jcf->cij", own_imag, real_part, preferred_element_type=jnp.float32)
        - jnp.einsum("icf,jcf->cij", own_real, imag_part, preferred_element_type=jnp.float32)
    ) * (1.0 / SPEC)
    visibilities = jnp.stack([vis_real, vis_imag], axis=1)
    beam_block = beam_weights.shape[2]
    own_groups = lax.dynamic_slice_in_dim(beam_group, block_index * beam_block, beam_block, 0)
    members = station_group[:, 0][None, :] == own_groups[:, None]
    scaling = 1.0 / jnp.sqrt(jnp.sum(members.astype(jnp.float32), axis=1))
    weights = jnp.where(members[None, None], beam_weights, jnp.zeros((), jnp.bfloat16))
    weight_real = weights[:, 0]
    imaginary_weight = weights[:, 1]
    beam_real = jnp.einsum(
        "cbs,scf->bcf", weight_real, real_part, preferred_element_type=jnp.float32
    ) - jnp.einsum("cbs,scf->bcf", imaginary_weight, imag_part, preferred_element_type=jnp.float32)
    beam_imag = jnp.einsum(
        "cbs,scf->bcf", weight_real, imag_part, preferred_element_type=jnp.float32
    ) + jnp.einsum("cbs,scf->bcf", imaginary_weight, real_part, preferred_element_type=jnp.float32)
    beams = (jnp.stack([beam_real, beam_imag], axis=1) * scaling[:, None, None, None]).astype(
        jnp.bfloat16
    )
    returned = lax.all_to_all(beams, "row", split_axis=0, concat_axis=2, tiled=True)
    inverse = jnp.einsum(
        "bqkf,qkpc->bpcf",
        returned.astype(jnp.float32),
        fourier_table(returned.shape[2], 1.0),
        precision=high,
    )
    beam_series = polyphase(inverse, synthesis_taps)
    return (visibilities, beam_series)


def solution(mesh):
    return jax.shard_map(
        body,
        mesh=mesh,
        in_specs=(
            P(("grp", "row", "col", "sub"), None, None, None),
            P(),
            P(),
            P("grp"),
            P("grp", None),
            P("grp"),
            P(("grp", "row"), None, ("col", "sub"), None),
        ),
        out_specs=(
            P("row", None, ("grp", "col", "sub"), None),
            P(("grp", "col", "sub", "row"), None, None, None),
        ),
        check_vma=False,
    )
```

profile of v0, /device:TPU:0, one launch (start us, length us, event | category | flops | bytes accessed | tf_op | source)
XLA Modules:
  0.0 157.8 jit_solution(14489460331540854039)
XLA Ops:
  7.4 1.2 slice.274
  8.5 1.2 slice.275
  9.7 0.1 slice.276
  9.8 0.1 slice.277
  10.0 0.1 slice.278
  10.1 0.1 slice.279
  10.2 0.1 slice.280
  10.4 0.1 slice.281
  10.5 0.1 slice.282
  10.6 0.1 slice.283
  10.8 0.1 slice.284
  10.9 0.1 slice.285
  11.0 0.1 slice.286
  11.2 0.1 slice.287
  11.3 0.1 slice.288
  11.4 0.2 copy-done.3
  11.6 5.1 %fusion.3 = bf16[16,2,16,512]{3,2,0,1:T(8,128)(2,1)S(1)} fusion(f32[16,2,16,497]{3,2,1,0:T(8,128)S(1)} %slice.288, f32[16,2,16,498]{3,2,1,0:T(8,128)S(1)} %slice.287, f32[16,2,16,499]{3,2,1,0:T(8,128)S(1)} %slice.286, f32[16,2,16,500]{3,2,1,0:T(8,128)S(1)} %slice.285, f32[16,2,16,501]{3,2,1,0:T(8,128)S(1)} %slice.284, f32[16,2,16,502]{3,2,1,0:T(8,128)S(1)} %slice.283, ...), kind=kOutput, calls=%fused_computation.11 | convolution fusion | flops 109316096 | bytes 16536576 | tf_op jit(solution)/shard_map/aqcf,qcpk->apkf/dot_general | solution.py:45
  16.8 0.3 copy.55
  17.1 20.6 %all_to_all.36 = bf16[16,2,16,512]{3,0,1,2:T(8,128)(2,1)S(1)} all-to-all(bf16[16,2,16,512]{3,0,1,2:T(8,128)(2,1)S(1)} %copy.55), channel_id=1, replica_groups=mesh['grp'=2,'row'=4,'col'=2,'sub'=2] {'row'}, dimensions={2} | all-to-all | bytes 1048576 | tf_op jit(solution)/shard_map/all_to_all | solution.py:48
  37.7 0.8 copy.57
  38.5 0.8 dynamic_slice.7
  39.3 0.1 convert_reduce_fusion
  39.4 1.9 %gather_fusion = s32[256]{0:T(256)S(1)} fusion(s32[256]{0:T(256)S(1)} %copy-done, s32[1024]{0:T(1024)S(1)} %pad_clamp_fusion), kind=kCustom, calls=%fused_computation | custom fusion | bytes 3072 | tf_op jit(solution)/shard_map/gather | solution.py:64
  41.4 0.1 broadcast_compare_fusion
  41.5 18.9 %all-gather.2.cloned.1.call-done = bf16[256,2,4,512]{3,0,2,1:T(8,128)(2,1)} async-done(((bf16[64,2,4,512]{3,0,2,1:T(8,128)(2,1)}), bf16[256,2,4,512]{3,0,2,1:T(8,128)(2,1)}) %all-gather.2.cloned.1.call-update) | async-done | bytes 2097168 | tf_op jit(solution)/shard_map/all_gather | solution.py:56
  60.4 2.8 %copy.58 = bf16[256,2,4,512]{0,3,2,1:T(8,128)(2,1)S(1)} copy(bf16[256,2,4,512]{3,0,2,1:T(8,128)(2,1)} %all-gather.2.cloned.1.call-done) | data formatting | bytes 4194304 | tf_op jit(solution)/shard_map/all_gather | solution.py:56
  63.2 0.7 fusion
  63.9 0.2 reshape.289
  64.1 0.1 fusion.103
  64.2 0.5 fusion.72
  64.6 0.5 fusion.75
  65.1 0.5 subtract_bitcast_fusion
  65.6 0.5 add_bitcast_fusion
  66.1 0.4 fusion.1
  66.6 3.1 %copy.64 = bf16[256,2,4,512]{3,2,1,0:T(4,128)(2,1)} copy(bf16[256,2,4,512]{0,3,2,1:T(8,128)(2,1)S(1)} %fusion.1) | data formatting | bytes 4194304 | tf_op jit(solution)/shard_map/convert_element_type | solution.py:99
  69.6 4.6 %all-to-all-start.1 = ((bf16[256,2,4,512]{3,2,1,0:T(4,128)(2,1)}), bf16[256,2,4,512]{3,2,1,0:T(4,128)(2,1)S(1)}, u32[]{:S(2)}, u32[]{:S(2)}) async-start(bf16[256,2,4,512]{3,2,1,0:T(4,128)(2,1)} %copy.64), calls=%async_computation.1 | async-start | bytes 4194304 | tf_op jit(solution)/shard_map/all_to_all | solution.py:102
  74.3 0.1 fusion.74
  74.5 0.2 fusion.7
  74.6 0.1 fusion.73
  74.8 0.2 fusion.5
  74.9 0.6 copy.67
  75.6 47.3 %all-to-all-done.1 = bf16[256,2,4,512]{3,2,1,0:T(4,128)(2,1)S(1)} async-done(((bf16[256,2,4,512]{3,2,1,0:T(4,128)(2,1)}), bf16[256,2,4,512]{3,2,1,0:T(4,128)(2,1)S(1)}, u32[]{:S(2)}, u32[]{:S(2)}) %all-to-all-start.1) | async-done | bytes 2097184 | tf_op jit(solution)/shard_map/all_to_all | solution.py:102
  122.8 0.7 copy.65
  123.5 2.9 %copy.66 = bf16[64,2,4,4,512]{4,3,2,1,0:T(4,128)(2,1)} copy(bf16[64,2,4,4,512]{4,0,2,3,1:T(8,128)(2,1)S(1)} %bitcast.188) | data formatting | bytes 4194304 | tf_op jit(solution)/shard_map/all_to_all | solution.py:102
  126.5 2.5 %reshape.302 = bf16[64,2,16,512,1]{3,2,1,0,4:T(8,128)(2,1)S(1)} reshape(bf16[64,2,4,4,512]{4,3,2,1,0:T(4,128)(2,1)} %copy.66) | data formatting | bytes 4194304 | tf_op jit(solution)/shard_map/all_to_all | solution.py:102
  129.0 2.0 %convolution_bitcast_fusion = f32[64,2,16,512]{3,2,0,1:T(8,128)S(1)} fusion(bf16[64,2,16,512,1]{3,2,1,0,4:T(8,128)(2,1)S(1)} %reshape.302, f32[1,2,16,16]{2,3,0,1:T(8,128)S(1)} %get-tuple-element.37, f32[1,2,16,16]{2,3,0,1:T(8,128)S(1)} %get-tuple-element.16), kind=kOutput, calls=%fused_computation.6 | convolution fusion | flops 402655232 | bytes 6295552 | tf_op jit(solution)/shard_map/bqkf,qkpc->bpcf/dot_general | solution.py:103
  131.0 17.3 %multiply_add_fusion = f32[64,2,16,512]{3,2,0,1:T(8,128)S(1)} fusion(f32[64,2,16,497]{3,2,0,1:T(8,128)S(1)} %bitcast.172, f32[64,2,16,498]{3,2,0,1:T(8,128)S(1)} %bitcast.173, f32[64,2,16,499]{3,2,0,1:T(8,128)S(1)} %bitcast.174, f32[64,2,16,500]{3,2,0,1:T(8,128)S(1)} %bitcast.175, f32[64,2,16,501]{3,2,0,1:T(8,128)S(1)} %bitcast.176, ...), kind=kLoop, calls=%fused_computation.5 | loop fusion | flops 32505856 | bytes 70321152 | tf_op jit(solution)/shard_map/add | solution.py:18
  148.4 2.6 %copy.68 = f32[64,2,16,512]{3,2,1,0:T(8,128)} copy(f32[64,2,16,512]{3,2,0,1:T(8,128)S(1)} %multiply_add_fusion) | data formatting | bytes 8388608
  (24 shorter events, 0.3 us)
Async XLA Ops:
  7.2 32.3 %copy-start = (s32[256]{0:T(256)S(1)}, s32[256]{0:T(256)}, u32[]{:S(2)}) copy-start(s32[256]{0:T(256)} %param.10) | copy-start | bytes 3076
  7.2 2.5 %copy-start.1 = (bf16[16,2,16,512]{3,2,1,0:T(8,128)(2,1)S(1)}, bf16[16,2,16,512]{3,2,1,0:T(8,128)(2,1)}, u32[]{:S(2)}) copy-start(bf16[16,2,16,512]{3,2,1,0:T(8,128)(2,1)} %param.7) | copy-start | bytes 1572868
  7.2 53.2 %all-gather.2.cloned.1.call-start = ((), (), s32[]{:S(2)}) async-start(), calls=%async_computation.2 | async-start | bytes 2621440 | tf_op jit(solution)/shard_map/all_gather | solution.py:56
  10.9 0.7 copy-start.3
  11.6 27.7 %copy-start.5 = (s32[32,1]{0,1:T(1,128)S(1)}, s32[32,1]{0,1:T(1,128)}, u32[]{:S(2)}) copy-start(s32[32,1]{0,1:T(1,128)} %param.11) | copy-start | bytes 388
  16.7 24.7 %copy-start.2 = (bf16[4,2,256,32]{2,3,1,0:T(8,128)(2,1)S(1)}, bf16[4,2,256,32]{2,3,1,0:T(8,128)(2,1)}, u32[]{:S(2)}) copy-start(bf16[4,2,256,32]{2,3,1,0:T(8,128)(2,1)} %param.13) | copy-start | bytes 393220
  66.5 7.7 %copy-start.4 = (f32[16,16]{1,0:T(8,128)S(1)}, f32[16,16]{1,0:T(8,128)}, u32[]{:S(2)}) copy-start(f32[16,16]{1,0:T(8,128)} %param.9) | copy-start | bytes 3076
  69.6 53.2 %all-to-all-start.1 = ((bf16[256,2,4,512]{3,2,1,0:T(4,128)(2,1)}), bf16[256,2,4,512]{3,2,1,0:T(4,128)(2,1)S(1)}, u32[]{:S(2)}, u32[]{:S(2)}) async-start(bf16[256,2,4,512]{3,2,1,0:T(4,128)(2,1)} %copy.64), calls=%async_computation.1 | async-start | bytes 4194304 | tf_op jit(solution)/shard_map/all_to_all | solution.py:102
Sparse Core Ops, SparseCore 0:
  38.6 21.6 all-gather.1
where the time goes:
time: 158 us
  waiting for transfers between devices  66.2 us (42%)
  local copies, waits for them, and re-layouts  23.5 us (15%)
  blocking collectives  20.6 us (13%)
  other arithmetic  18.1 us (11%)
  between operations  14.4 us (9%)
  matrix products  10.3 us (7%)
  starting transfers between devices  4.66 us (3%)
    all_to_all x1, waiting for transfers between devices, body(): lax.all_to_all(beams, 'row', split_axis=0, concat_axis=2, tiled=True)  47.3 us
    all_to_all x1, blocking collectives, body(): lax.all_to_all(spectra, 'row', split_axis=2, concat_axis=0, tiled=True)  20.6 us
    all_gather x1, waiting for transfers between devices, body(): shard_rows = lax.all_gather(turned, ('col', 'sub'), axis=0, tiled=True)  18.9 us
    add x1, other arithmetic, polyphase(): output = output + coefficients[tap_index][:, None] * shifted  17.3 us
    all_to_all x3, local copies, waits for them, and re-layouts, body(): lax.all_to_all(beams, 'row', split_axis=0, concat_axis=2, tiled=True)  6.19 us
    dot_general x1, matrix products, body(): jnp.einsum('aqcf,qcpk->apkf', filtered, fourier_table(samples.shape[2], -...  5.12 us
    all_to_all x1, starting transfers between devices, body(): lax.all_to_all(beams, 'row', split_axis=0, concat_axis=2, tiled=True)  4.62 us
    slice x15, local copies, waits for them, and re-layouts, polyphase(): signal[..., :length - tap_index]  3.91 us
  transfers between devices with their start and end apart: 2, of which 2 were waited for; matrix products, arithmetic and copies ran while one was open for 3% of the time, Pallas kernels for 0%

commit v1 on v0

--- a/solution.py
+++ b/solution.py
@@ -99,7 +99,10 @@
     beams = (jnp.stack([beam_real, beam_imag], axis=1) * scaling[:, None, None, None]).astype(
         jnp.bfloat16
     )
-    returned = lax.all_to_all(beams, "row", split_axis=0, concat_axis=2, tiled=True)
+    returned = jnp.concatenate(
+        lax.all_to_all(jnp.stack(jnp.split(beams, lax.axis_size("row"), axis=0)), "row", 0, 0),
+        axis=2,
+    )
     inverse = jnp.einsum(
         "bqkf,qkpc->bpcf",
         returned.astype(jnp.float32),

time: 158 us -> 152 us (0.962)
  local copies, waits for them, and re-layouts: 23.5 us -> 14.6 us
  other arithmetic: 18.1 us -> 19.9 us
    all_to_all x3 -> x0, local copies, waits for them, and re-layouts: 6.19 us -> none  [body(): lax.all_to_all(beams, 'row', split_axis=0, concat_axis=2, tiled=True)]
    convert_element_type x1 -> x0, local copies, waits for them, and re-layouts: 3.08 us -> none  [body(): (jnp.stack([beam_real, beam_imag], axis=1) * scaling[:, None, None, None]...]
    another operation x0 -> x1, other arithmetic: none -> 1.58 us  [body(): jnp.stack(jnp.split(beams, lax.axis_size('row'), axis=0))]
where the time goes in v1:
time: 152 us; the launch traced here: 151 us
  waiting for transfers between devices  66.2 us (44%)
  blocking collectives  20.6 us (14%)
  other arithmetic  19.9 us (13%)
  local copies, waits for them, and re-layouts  14.6 us (10%)
  between operations  14.4 us (9%)
  matrix products  11 us (7%)
  starting transfers between devices  4.63 us (3%)
    all_to_all x1, waiting for transfers between devices, body(): lax.all_to_all(jnp.stack(jnp.split(beams, lax.axis_size('row'), axis=0)),...  47.3 us
    all_to_all x1, blocking collectives, body(): lax.all_to_all(spectra, 'row', split_axis=2, concat_axis=0, tiled=True)  20.6 us
    all_gather x1, waiting for transfers between devices, body(): shard_rows = lax.all_gather(turned, ('col', 'sub'), axis=0, tiled=True)  18.9 us
    add x1, other arithmetic, polyphase(): output = output + coefficients[tap_index][:, None] * shifted  17.3 us
    dot_general x1, matrix products, body(): jnp.einsum('aqcf,qcpk->apkf', filtered, fourier_table(samples.shape[2], -...  5.12 us
    all_to_all x1, starting transfers between devices, body(): lax.all_to_all(jnp.stack(jnp.split(beams, lax.axis_size('row'), axis=0)),...  4.59 us
    slice x15, local copies, waits for them, and re-layouts, polyphase(): signal[..., :length - tap_index]  3.95 us
    unnamed x14, local copies, waits for them, and re-layouts  3.39 us
  transfers between devices with their start and end apart: 2, of which 2 were waited for; matrix products, arithmetic and copies ran while one was open for 3% of the time, Pallas kernels for 0%

profile of v1, /device:TPU:0, one launch (start us, length us, event | category | flops | bytes accessed | tf_op | source)
XLA Modules:
  0.0 151.4 jit_solution(508741926521402387)
XLA Ops:
  7.2 0.1 broadcast_multiply_fusion
  7.4 1.2 slice.274
  8.5 1.2 slice.275
  9.7 0.1 slice.276
  9.8 0.1 slice.277
  10.0 0.1 slice.278
  10.1 0.1 slice.279
  10.2 0.1 slice.280
  10.4 0.1 slice.281
  10.5 0.1 slice.282
  10.6 0.1 slice.283
  10.8 0.1 slice.284
  10.9 0.1 slice.285
  11.1 0.1 slice.286
  11.2 0.1 slice.287
  11.3 0.1 slice.288
  11.5 0.2 copy-done.3
  11.6 5.1 %fusion.5 = bf16[16,2,16,512]{3,2,0,1:T(8,128)(2,1)S(1)} fusion(f32[16,2,16,497]{3,2,1,0:T(8,128)S(1)} %slice.288, f32[16,2,16,498]{3,2,1,0:T(8,128)S(1)} %slice.287, f32[16,2,16,499]{3,2,1,0:T(8,128)S(1)} %slice.286, f32[16,2,16,500]{3,2,1,0:T(8,128)S(1)} %slice.285, f32[16,2,16,501]{3,2,1,0:T(8,128)S(1)} %slice.284, f32[16,2,16,502]{3,2,1,0:T(8,128)S(1)} %slice.283, ...), kind=kOutput, calls=%fused_computation.14 | convolution fusion | flops 109316096 | bytes 16536576 | tf_op jit(solution)/shard_map/aqcf,qcpk->apkf/dot_general | solution.py:45
  16.8 0.3 copy.53
  17.1 20.6 %all_to_all.23 = bf16[16,2,16,512]{3,0,1,2:T(8,128)(2,1)S(1)} all-to-all(bf16[16,2,16,512]{3,0,1,2:T(8,128)(2,1)S(1)} %copy.53), channel_id=1, replica_groups=mesh['grp'=2,'row'=4,'col'=2,'sub'=2] {'row'}, dimensions={2} | all-to-all | bytes 1048576 | tf_op jit(solution)/shard_map/all_to_all | solution.py:48
  37.7 0.8 copy.55
  38.6 0.8 dynamic_slice.7
  39.3 0.1 convert_reduce_fusion
  39.5 1.9 %gather_fusion = s32[256]{0:T(256)S(1)} fusion(s32[256]{0:T(256)S(1)} %copy-done, s32[1024]{0:T(1024)S(1)} %pad_clamp_fusion), kind=kCustom, calls=%fused_computation | custom fusion | bytes 3072 | tf_op jit(solution)/shard_map/gather | solution.py:64
  41.4 0.1 broadcast_compare_fusion
  41.5 18.9 %all-gather.2.cloned.1.call-done = bf16[256,2,4,512]{3,0,2,1:T(8,128)(2,1)} async-done(((bf16[64,2,4,512]{3,0,2,1:T(8,128)(2,1)}), bf16[256,2,4,512]{3,0,2,1:T(8,128)(2,1)}) %all-gather.2.cloned.1.call-update) | async-done | bytes 2097168 | tf_op jit(solution)/shard_map/all_gather | solution.py:56
  60.4 2.8 %copy.56 = bf16[256,2,4,512]{0,3,2,1:T(8,128)(2,1)S(1)} copy(bf16[256,2,4,512]{3,0,2,1:T(8,128)(2,1)} %all-gather.2.cloned.1.call-done) | data formatting | bytes 4194304 | tf_op jit(solution)/shard_map/all_gather | solution.py:56
  63.2 0.7 fusion
  63.9 0.2 reshape.295
  64.1 0.1 fusion.105
  64.2 0.5 fusion.74
  64.7 0.5 fusion.77
  65.1 0.5 subtract_bitcast_fusion
  65.6 0.5 add_bitcast_fusion
  66.1 0.7 fusion.1
  66.8 0.2 slice_bitcast_fusion.3
  67.1 1.6 %pad_maximum_fusion = bf16[4,64,2,4,512]{4,1,3,2,0:T(8,128)(2,1)} fusion(bf16[1,64,2,4,512]{4,1,3,2,0:T(8,128)(2,1)S(1)} %get-tuple-element.13, bf16[1,64,2,4,512]{4,1,3,2,0:T(8,128)(2,1)S(1)} %get-tuple-element.14, bf16[1,64,2,4,512]{4,1,3,2,0:T(8,128)(2,1)S(1)} %get-tuple-element.15, bf16[1,64,2,4,512]{4,1,3,2,0:T(8,128)(2,1)S(1)} %get-tuple-element.12), kind=kLoop, calls=%fused_computation.7 | loop fusion | flops 3145728 | bytes 4194304 | tf_op jit(solution)/shard_map/stack | solution.py:103
  68.6 4.6 %all-to-all-start.1 = ((bf16[4,64,2,4,512]{4,1,3,2,0:T(8,128)(2,1)}), bf16[4,64,2,4,512]{4,1,3,2,0:T(8,128)(2,1)S(1)}, u32[]{:S(2)}, u32[]{:S(2)}) async-start(bf16[4,64,2,4,512]{4,1,3,2,0:T(8,128)(2,1)} %pad_maximum_fusion), calls=%async_computation.1 | async-start | bytes 4194304 | tf_op jit(solution)/shard_map/all_to_all | solution.py:103
  73.3 0.1 fusion.76
  73.4 0.2 fusion.9
  73.6 0.1 fusion.75
  73.7 0.2 fusion.7
  73.9 0.6 copy.64
  74.5 47.3 %all-to-all-done.1 = bf16[4,64,2,4,512]{4,1,3,2,0:T(8,128)(2,1)S(1)} async-done(((bf16[4,64,2,4,512]{4,1,3,2,0:T(8,128)(2,1)}), bf16[4,64,2,4,512]{4,1,3,2,0:T(8,128)(2,1)S(1)}, u32[]{:S(2)}, u32[]{:S(2)}) %all-to-all-start.1) | async-done | bytes 2097184 | tf_op jit(solution)/shard_map/all_to_all | solution.py:103
  121.8 0.1 copy.62
  122.0 2.7 %convolution_bitcast_fusion = f32[64,2,16,512]{3,2,0,1:T(8,128)S(1)} fusion(bf16[64,2,16,512]{3,0,2,1:T(8,128)(2,1)S(1)} %bitcast.196, f32[1,2,16,16]{2,3,0,1:T(8,128)S(1)} %get-tuple-element.41, f32[1,2,16,16]{2,3,0,1:T(8,128)S(1)} %get-tuple-element.20), kind=kOutput, calls=%fused_computation.6 | convolution fusion | flops 402655232 | bytes 6295552 | tf_op jit(solution)/shard_map/bqkf,qkpc->bpcf/dot_general | solution.py:106
  124.7 17.3 %multiply_add_fusion = f32[64,2,16,512]{3,2,0,1:T(8,128)S(1)} fusion(f32[64,2,16,497]{3,2,0,1:T(8,128)S(1)} %bitcast.181, f32[64,2,16,498]{3,2,0,1:T(8,128)S(1)} %bitcast.182, f32[64,2,16,499]{3,2,0,1:T(8,128)S(1)} %bitcast.183, f32[64,2,16,500]{3,2,0,1:T(8,128)S(1)} %bitcast.184, f32[64,2,16,501]{3,2,0,1:T(8,128)S(1)} %bitcast.185, ...), kind=kLoop, calls=%fused_computation.5 | loop fusion | flops 32505856 | bytes 70321152 | tf_op jit(solution)/shard_map/add | solution.py:18
  142.0 2.6 %copy.65 = f32[64,2,16,512]{3,2,1,0:T(8,128)} copy(f32[64,2,16,512]{3,2,0,1:T(8,128)S(1)} %multiply_add_fusion) | data formatting | bytes 8388608
  (23 shorter events, 0.3 us)
Async XLA Ops:
  7.2 32.3 %copy-start = (s32[256]{0:T(256)S(1)}, s32[256]{0:T(256)}, u32[]{:S(2)}) copy-start(s32[256]{0:T(256)} %param.10) | copy-start | bytes 3076
  7.2 2.5 %copy-start.1 = (bf16[16,2,16,512]{3,2,1,0:T(8,128)(2,1)S(1)}, bf16[16,2,16,512]{3,2,1,0:T(8,128)(2,1)}, u32[]{:S(2)}) copy-start(bf16[16,2,16,512]{3,2,1,0:T(8,128)(2,1)} %param.7) | copy-start | bytes 1572868
  7.2 53.2 %all-gather.2.cloned.1.call-start = ((), (), s32[]{:S(2)}) async-start(), calls=%async_computation.2 | async-start | bytes 2621440 | tf_op jit(solution)/shard_map/all_gather | solution.py:56
  10.9 0.7 copy-start.3
  11.6 27.7 %copy-start.5 = (s32[32,1]{0,1:T(1,128)S(1)}, s32[32,1]{0,1:T(1,128)}, u32[]{:S(2)}) copy-start(s32[32,1]{0,1:T(1,128)} %param.11) | copy-start | bytes 388
  16.8 24.7 %copy-start.2 = (bf16[4,2,256,32]{2,3,1,0:T(8,128)(2,1)S(1)}, bf16[4,2,256,32]{2,3,1,0:T(8,128)(2,1)}, u32[]{:S(2)}) copy-start(bf16[4,2,256,32]{2,3,1,0:T(8,128)(2,1)} %param.13) | copy-start | bytes 393220
  67.1 6.2 %copy-start.4 = (f32[16,16]{1,0:T(8,128)S(1)}, f32[16,16]{1,0:T(8,128)}, u32[]{:S(2)}) copy-start(f32[16,16]{1,0:T(8,128)} %param.9) | copy-start | bytes 3076
  68.6 53.2 %all-to-all-start.1 = ((bf16[4,64,2,4,512]{4,1,3,2,0:T(8,128)(2,1)}), bf16[4,64,2,4,512]{4,1,3,2,0:T(8,128)(2,1)S(1)}, u32[]{:S(2)}, u32[]{:S(2)}) async-start(bf16[4,64,2,4,512]{4,1,3,2,0:T(8,128)(2,1)} %pad_maximum_fusion), calls=%async_computation.1 | async-start | bytes 4194304 | tf_op jit(solution)/shard_map/all_to_all | solution.py:103
Sparse Core Ops, SparseCore 0:
  38.7 21.6 all-gather.1
